TPU v7x, 256 devices: a whole 4x4x8 slice. The times are simulated.
256 devices in a mesh: slot: 32 (over z_hi, y, core), tp: 8 (over z_lo, x).
Axes of the slice: x: 4, y: 4, z: 8 (z_hi: 4, z_lo: 2; z = z_hi * 2 + z_lo), core: 2. Of those that a mesh axis runs over, the one named last changes fastest.
Arguments:
- hidden: bfloat16 [14336, 6144], P('slot', 'tp'), may hold values from -4 to 4
- queries: bfloat16 [14336, 3072], P('slot', 'tp'), may hold values from -22 to 22
- key_rows: bfloat16 [14336, 3072], P('slot', 'tp'), may hold values from -6 to 6
- values: bfloat16 [14336, 3072], P('slot', 'tp'), may hold values from -6 to 6
- out_weight: bfloat16 [3072, 6144], P('tp'), may hold values from -0.109375 to 0.109375
- level_table: float32 [64, 6144], P(None, 'tp'), may hold values from 0.3 to 3
- noise_level: int32 [32], P('slot'), may hold values from 0 to 63
- group_live: int32 [32], replicated, may hold values 0 or 1
Outputs:
- refined: bfloat16 [14336, 6144], P('slot', 'tp')
All inputs are finite; a program needn't handle non-finite values.
Results may differ from a plain program's by a relative error of at most 0.014.
Values may be sent and summed in bfloat16 or wider, within the bound.
No kernel may reach another device: no remote copies, remote signals or barrier semaphores. Data moves between devices by JAX's collectives and lax.ppermute only.
A program may use at most 128 MiB of HBM per device.

v0:
```python
import math

import jax
import jax.numpy as jnp
from jax import lax
from jax.sharding import PartitionSpec as P

HD = 128


def passed_along(value, axis, steps):
    count = lax.axis_size(axis)
    pairs = [(source, (source + steps) % count) for source in range(count)]
    return lax.ppermute(value, axis, pairs)


def per_device(hidden, queries, key_rows, values, out_weight, level_table, noise_level, group_live):
    group_rows = queries.shape[0]
    width = queries.shape[1]
    heads_here = width // HD
    own_slot = lax.axis_index("slot")
    score_scale = HD ** (-0.5)
    query_heads = queries.reshape(group_rows, heads_here, HD)
    slot_ids = jnp.arange(group_live.shape[0], dtype=jnp.int32)

    def absorb(carry, key_block, value_block, first):
        row_max, row_sum, weighted = carry
        span_len = key_block.shape[0]
        key_heads = key_block.reshape(span_len, heads_here, HD)
        value_heads = value_block.reshape(span_len, heads_here, HD)
        scores = (
            jnp.einsum("qhd,khd->hqk", query_heads, key_heads, preferred_element_type=jnp.float32)
            * score_scale
        )
        group_of = (first + jnp.arange(span_len, dtype=jnp.int32)) // group_rows
        alive_flag = jnp.sum(
            jnp.where(group_of[:, None] == slot_ids[None, :], group_live[None, :], 0), axis=1
        )
        allowed = (
            (group_of >= 0) & (group_of <= own_slot) & ((alive_flag == 1) | (group_of == own_slot))
        )
        masked = jnp.where(allowed[None, None, :], scores, -1e30)
        new_max = jnp.maximum(row_max, jnp.max(masked, axis=2))
        expon = jnp.where(allowed[None, None, :], jnp.exp(scores - new_max[..., None]), 0.0)
        shrink = jnp.exp(row_max - new_max)
        row_sum = row_sum * shrink + jnp.sum(expon, axis=2)
        weighted = weighted * shrink[..., None] + jnp.einsum(
            "hqk,khd->hqd",
            expon.astype(jnp.bfloat16),
            value_heads,
            preferred_element_type=jnp.float32,
        )
        return (new_max, row_sum, weighted)

    initial = (
        jnp.full((heads_here, group_rows), -1e30, jnp.float32),
        jnp.zeros((heads_here, group_rows), jnp.float32),
        jnp.zeros((heads_here, group_rows, HD), jnp.float32),
    )
    carry = initial
    key_piece = lax.all_gather(key_rows, "slot", axis=0, tiled=True)
    value_piece = lax.all_gather(values, "slot", axis=0, tiled=True)
    span_len = key_piece.shape[0]
    span_block = math.gcd(span_len, 4 * group_rows)
    block_total = span_len // span_block
    key_blocks = key_piece.reshape(block_total, span_block, width)
    value_blocks = value_piece.reshape(block_total, span_block, width)

    def advance(state, entry):
        key_block, value_block, position = entry
        return (absorb(state, key_block, value_block, position * span_block), None)

    carry, unused = lax.scan(
        advance, carry, (key_blocks, value_blocks, jnp.arange(block_total, dtype=jnp.int32))
    )
    row_max, row_sum, weighted = carry
    attended = (
        (weighted / row_sum[..., None])
        .astype(jnp.bfloat16)
        .transpose(1, 0, 2)
        .reshape(group_rows, width)
    )
    partial_value = jnp.dot(attended, out_weight, preferred_element_type=jnp.float32)
    projected = lax.psum_scatter(
        partial_value.astype(jnp.bfloat16), "tp", scatter_dimension=1, tiled=True
    ).astype(jnp.float32)
    picked = jnp.arange(level_table.shape[0], dtype=jnp.int32) == noise_level[0]
    gate_row = jnp.sum(jnp.where(picked[:, None], level_table, 0.0), axis=0)
    mixed_out = (hidden.astype(jnp.float32) + gate_row[None, :] * projected).astype(jnp.bfloat16)
    return passed_along(mixed_out, "slot", -1)


def solution(mesh):
    in_specs = (
        P("slot", "tp"),
        P("slot", "tp"),
        P("slot", "tp"),
        P("slot", "tp"),
        P("tp", None),
        P(None, "tp"),
        P("slot"),
        P(),
    )
    out_specs = P("slot", "tp")
    return jax.shard_map(
        per_device, mesh=mesh, in_specs=in_specs, out_specs=out_specs, check_vma=False
    )
```

profile of v0, /device:TPU:25, one launch (start us, length us, event | category | flops | bytes accessed | tf_op | source)
XLA Modules:
  0.0 505.9 jit_solution(936888661831730769)
XLA Ops:
  9.5 95.3 %all-gather.3.cloned.1.call-done = bf16[14336,384]{1,0:T(8,128)(2,1)} async-done(((bf16[448,384]{1,0:T(8,128)(2,1)}), bf16[14336,384]{1,0:T(8,128)(2,1)}) %all-gather.3.cloned.1.call-update) | async-done | bytes 11010064 | tf_op jit(solution)/shard_map/all_gather | solution.py:61
  104.8 92.9 %all-gather.5.cloned.1.call-done = bf16[14336,384]{1,0:T(8,128)(2,1)} async-done(((bf16[448,384]{1,0:T(8,128)(2,1)}), bf16[14336,384]{1,0:T(8,128)(2,1)}) %all-gather.5.cloned.1.call-update) | async-done | bytes 11010064 | tf_op jit(solution)/shard_map/all_gather | solution.py:62
  197.6 202.9 %while.17 = (s32[]{:T(128)}, f32[3,448]{1,0:T(4,128)S(1)}, f32[3,448]{1,0:T(4,128)S(1)}, f32[3,448,128]{2,1,0:T(8,128)}, s32[8]{0:T(128)S(1)}, /*index=5*/s32[]{...) while((s32[]{:T(128)}, f32[3,448]{1,0:T(4,128)S(1)}, ...), condition=%wide.region_5.6_spmd.clone, body=%wide.region_1.5_spmd.clone.sunk | while | flops 1260356096 | bytes 44506412 | solution.py:73
  199.6 3.2 constant_dynamic-slice_fusion.3
  202.7 1.8 copy.34
  204.6 5.2 %select_reduce_fusion.6 = (f32[3,448]{1,0:T(4,128)S(1)}, f32[3,1792,448]{1,2,0:T(8,128)}) fusion(pred[1792]{0:T(1024)(128)(4,1)S(1)} %or_and_fusion.2, bf16[448,3,128]{2,0,1:T(8,128)(2,1)S(1)} %get-tuple-element.344, bf16[1792,3,128]{0,2,1:T(8,128)(2,1)S(1)} %bitcast.38), kind=kOutput, calls=%fused_computation.4.clone.1 | convolution fusion | flops 623786688 | bytes 11361280 | tf_op jit(solution)/shard_map/while/body/eval_jaxpr/qhd,khd->hqk/dot_general | solution.py:32
  209.8 5.8 %bitcast_reduce_fusion.2 = f32[3,448]{1,0:T(4,128)S(1)} fusion(f32[3,1792,448]{1,2,0:T(8,128)} %get-tuple-element.306, f32[3,448]{1,0:T(4,128)S(1)} %select_maximum_fusion.2, pred[1792]{0:T(1024)(128)(4,1)S(1)} %or_and_fusion.2), kind=kLoop, calls=%fused_computation.2.clone.1 | loop fusion | flops 9632448 | bytes 9646336 | tf_op jit(solution)/shard_map/while/body/eval_jaxpr/reduce_sum | solution.py:46
  216.5 6.4 %fusion.24 = f32[3,448,128]{2,1,0:T(8,128)} fusion(bf16[1792,3,128]{0,2,1:T(8,128)(2,1)S(1)} %bitcast.39, f32[3,1792,448]{1,2,0:T(8,128)} %get-tuple-element.306, f32[3,448]{1,0:T(4,128)S(1)} %select_maximum_fusion.2, pred[1792]{0:T(1024)(128)(4,1)S(1)} %or_and_fusion.2, f32[3,448,128]{2,1,0:T(8,128)} %get-tuple-element.326, ...), kind=kOutput, calls=%fused_computation.7.clone.1 | convolution fusion | flops 626712576 | bytes 12398849 | tf_op jit(solution)/shard_map/while/body/eval_jaxpr/hqk,khd->hqd/dot_general | solution.py:47
  224.8 3.2 constant_dynamic-slice_fusion.3
  228.0 1.8 copy.34
  229.8 5.2 %select_reduce_fusion.6 = (f32[3,448]{1,0:T(4,128)S(1)}, f32[3,1792,448]{1,2,0:T(8,128)}) fusion(pred[1792]{0:T(1024)(128)(4,1)S(1)} %or_and_fusion.2, bf16[448,3,128]{2,0,1:T(8,128)(2,1)S(1)} %get-tuple-element.344, bf16[1792,3,128]{0,2,1:T(8,128)(2,1)S(1)} %bitcast.38), kind=kOutput, calls=%fused_computation.4.clone.1 | convolution fusion | flops 623786688 | bytes 11361280 | tf_op jit(solution)/shard_map/while/body/eval_jaxpr/qhd,khd->hqk/dot_general | solution.py:32
  235.1 5.8 %bitcast_reduce_fusion.2 = f32[3,448]{1,0:T(4,128)S(1)} fusion(f32[3,1792,448]{1,2,0:T(8,128)} %get-tuple-element.306, f32[3,448]{1,0:T(4,128)S(1)} %select_maximum_fusion.2, pred[1792]{0:T(1024)(128)(4,1)S(1)} %or_and_fusion.2), kind=kLoop, calls=%fused_computation.2.clone.1 | loop fusion | flops 9632448 | bytes 9646336 | tf_op jit(solution)/shard_map/while/body/eval_jaxpr/reduce_sum | solution.py:46
  241.7 6.5 %fusion.24 = f32[3,448,128]{2,1,0:T(8,128)} fusion(bf16[1792,3,128]{0,2,1:T(8,128)(2,1)S(1)} %bitcast.39, f32[3,1792,448]{1,2,0:T(8,128)} %get-tuple-element.306, f32[3,448]{1,0:T(4,128)S(1)} %select_maximum_fusion.2, pred[1792]{0:T(1024)(128)(4,1)S(1)} %or_and_fusion.2, f32[3,448,128]{2,1,0:T(8,128)} %get-tuple-element.326, ...), kind=kOutput, calls=%fused_computation.7.clone.1 | convolution fusion | flops 626712576 | bytes 12398849 | tf_op jit(solution)/shard_map/while/body/eval_jaxpr/hqk,khd->hqd/dot_general | solution.py:47
  250.2 3.2 constant_dynamic-slice_fusion.3
  253.4 1.8 copy.34
  255.2 5.2 %select_reduce_fusion.6 = (f32[3,448]{1,0:T(4,128)S(1)}, f32[3,1792,448]{1,2,0:T(8,128)}) fusion(pred[1792]{0:T(1024)(128)(4,1)S(1)} %or_and_fusion.2, bf16[448,3,128]{2,0,1:T(8,128)(2,1)S(1)} %get-tuple-element.344, bf16[1792,3,128]{0,2,1:T(8,128)(2,1)S(1)} %bitcast.38), kind=kOutput, calls=%fused_computation.4.clone.1 | convolution fusion | flops 623786688 | bytes 11361280 | tf_op jit(solution)/shard_map/while/body/eval_jaxpr/qhd,khd->hqk/dot_general | solution.py:32
  260.4 5.8 %bitcast_reduce_fusion.2 = f32[3,448]{1,0:T(4,128)S(1)} fusion(f32[3,1792,448]{1,2,0:T(8,128)} %get-tuple-element.306, f32[3,448]{1,0:T(4,128)S(1)} %select_maximum_fusion.2, pred[1792]{0:T(1024)(128)(4,1)S(1)} %or_and_fusion.2), kind=kLoop, calls=%fused_computation.2.clone.1 | loop fusion | flops 9632448 | bytes 9646336 | tf_op jit(solution)/shard_map/while/body/eval_jaxpr/reduce_sum | solution.py:46
  267.1 6.5 %fusion.24 = f32[3,448,128]{2,1,0:T(8,128)} fusion(bf16[1792,3,128]{0,2,1:T(8,128)(2,1)S(1)} %bitcast.39, f32[3,1792,448]{1,2,0:T(8,128)} %get-tuple-element.306, f32[3,448]{1,0:T(4,128)S(1)} %select_maximum_fusion.2, pred[1792]{0:T(1024)(128)(4,1)S(1)} %or_and_fusion.2, f32[3,448,128]{2,1,0:T(8,128)} %get-tuple-element.326, ...), kind=kOutput, calls=%fused_computation.7.clone.1 | convolution fusion | flops 626712576 | bytes 12398849 | tf_op jit(solution)/shard_map/while/body/eval_jaxpr/hqk,khd->hqd/dot_general | solution.py:47
  275.6 3.2 constant_dynamic-slice_fusion.3
  278.8 1.8 copy.34
  280.6 5.3 %select_reduce_fusion.6 = (f32[3,448]{1,0:T(4,128)S(1)}, f32[3,1792,448]{1,2,0:T(8,128)}) fusion(pred[1792]{0:T(1024)(128)(4,1)S(1)} %or_and_fusion.2, bf16[448,3,128]{2,0,1:T(8,128)(2,1)S(1)} %get-tuple-element.344, bf16[1792,3,128]{0,2,1:T(8,128)(2,1)S(1)} %bitcast.38), kind=kOutput, calls=%fused_computation.4.clone.1 | convolution fusion | flops 623786688 | bytes 11361280 | tf_op jit(solution)/shard_map/while/body/eval_jaxpr/qhd,khd->hqk/dot_general | solution.py:32
  285.8 5.8 %bitcast_reduce_fusion.2 = f32[3,448]{1,0:T(4,128)S(1)} fusion(f32[3,1792,448]{1,2,0:T(8,128)} %get-tuple-element.306, f32[3,448]{1,0:T(4,128)S(1)} %select_maximum_fusion.2, pred[1792]{0:T(1024)(128)(4,1)S(1)} %or_and_fusion.2), kind=kLoop, calls=%fused_computation.2.clone.1 | loop fusion | flops 9632448 | bytes 9646336 | tf_op jit(solution)/shard_map/while/body/eval_jaxpr/reduce_sum | solution.py:46
  292.5 6.5 %fusion.24 = f32[3,448,128]{2,1,0:T(8,128)} fusion(bf16[1792,3,128]{0,2,1:T(8,128)(2,1)S(1)} %bitcast.39, f32[3,1792,448]{1,2,0:T(8,128)} %get-tuple-element.306, f32[3,448]{1,0:T(4,128)S(1)} %select_maximum_fusion.2, pred[1792]{0:T(1024)(128)(4,1)S(1)} %or_and_fusion.2, f32[3,448,128]{2,1,0:T(8,128)} %get-tuple-element.326, ...), kind=kOutput, calls=%fused_computation.7.clone.1 | convolution fusion | flops 626712576 | bytes 12398849 | tf_op jit(solution)/shard_map/while/body/eval_jaxpr/hqk,khd->hqd/dot_general | solution.py:47
  301.0 3.2 constant_dynamic-slice_fusion.3
  304.1 1.8 copy.34
  305.9 5.2 %select_reduce_fusion.6 = (f32[3,448]{1,0:T(4,128)S(1)}, f32[3,1792,448]{1,2,0:T(8,128)}) fusion(pred[1792]{0:T(1024)(128)(4,1)S(1)} %or_and_fusion.2, bf16[448,3,128]{2,0,1:T(8,128)(2,1)S(1)} %get-tuple-element.344, bf16[1792,3,128]{0,2,1:T(8,128)(2,1)S(1)} %bitcast.38), kind=kOutput, calls=%fused_computation.4.clone.1 | convolution fusion | flops 623786688 | bytes 11361280 | tf_op jit(solution)/shard_map/while/body/eval_jaxpr/qhd,khd->hqk/dot_general | solution.py:32
  311.2 5.8 %bitcast_reduce_fusion.2 = f32[3,448]{1,0:T(4,128)S(1)} fusion(f32[3,1792,448]{1,2,0:T(8,128)} %get-tuple-element.306, f32[3,448]{1,0:T(4,128)S(1)} %select_maximum_fusion.2, pred[1792]{0:T(1024)(128)(4,1)S(1)} %or_and_fusion.2), kind=kLoop, calls=%fused_computation.2.clone.1 | loop fusion | flops 9632448 | bytes 9646336 | tf_op jit(solution)/shard_map/while/body/eval_jaxpr/reduce_sum | solution.py:46
  317.9 6.5 %fusion.24 = f32[3,448,128]{2,1,0:T(8,128)} fusion(bf16[1792,3,128]{0,2,1:T(8,128)(2,1)S(1)} %bitcast.39, f32[3,1792,448]{1,2,0:T(8,128)} %get-tuple-element.306, f32[3,448]{1,0:T(4,128)S(1)} %select_maximum_fusion.2, pred[1792]{0:T(1024)(128)(4,1)S(1)} %or_and_fusion.2, f32[3,448,128]{2,1,0:T(8,128)} %get-tuple-element.326, ...), kind=kOutput, calls=%fused_computation.7.clone.1 | convolution fusion | flops 626712576 | bytes 12398849 | tf_op jit(solution)/shard_map/while/body/eval_jaxpr/hqk,khd->hqd/dot_general | solution.py:47
  326.4 3.2 constant_dynamic-slice_fusion.3
  329.5 1.8 copy.34
  331.3 5.3 %select_reduce_fusion.6 = (f32[3,448]{1,0:T(4,128)S(1)}, f32[3,1792,448]{1,2,0:T(8,128)}) fusion(pred[1792]{0:T(1024)(128)(4,1)S(1)} %or_and_fusion.2, bf16[448,3,128]{2,0,1:T(8,128)(2,1)S(1)} %get-tuple-element.344, bf16[1792,3,128]{0,2,1:T(8,128)(2,1)S(1)} %bitcast.38), kind=kOutput, calls=%fused_computation.4.clone.1 | convolution fusion | flops 623786688 | bytes 11361280 | tf_op jit(solution)/shard_map/while/body/eval_jaxpr/qhd,khd->hqk/dot_general | solution.py:32
  336.6 5.8 %bitcast_reduce_fusion.2 = f32[3,448]{1,0:T(4,128)S(1)} fusion(f32[3,1792,448]{1,2,0:T(8,128)} %get-tuple-element.306, f32[3,448]{1,0:T(4,128)S(1)} %select_maximum_fusion.2, pred[1792]{0:T(1024)(128)(4,1)S(1)} %or_and_fusion.2), kind=kLoop, calls=%fused_computation.2.clone.1 | loop fusion | flops 9632448 | bytes 9646336 | tf_op jit(solution)/shard_map/while/body/eval_jaxpr/reduce_sum | solution.py:46
  343.2 6.5 %fusion.24 = f32[3,448,128]{2,1,0:T(8,128)} fusion(bf16[1792,3,128]{0,2,1:T(8,128)(2,1)S(1)} %bitcast.39, f32[3,1792,448]{1,2,0:T(8,128)} %get-tuple-element.306, f32[3,448]{1,0:T(4,128)S(1)} %select_maximum_fusion.2, pred[1792]{0:T(1024)(128)(4,1)S(1)} %or_and_fusion.2, f32[3,448,128]{2,1,0:T(8,128)} %get-tuple-element.326, ...), kind=kOutput, calls=%fused_computation.7.clone.1 | convolution fusion | flops 626712576 | bytes 12398849 | tf_op jit(solution)/shard_map/while/body/eval_jaxpr/hqk,khd->hqd/dot_general | solution.py:47
  351.7 3.2 constant_dynamic-slice_fusion.3
  354.9 1.8 copy.34
  356.7 5.2 %select_reduce_fusion.6 = (f32[3,448]{1,0:T(4,128)S(1)}, f32[3,1792,448]{1,2,0:T(8,128)}) fusion(pred[1792]{0:T(1024)(128)(4,1)S(1)} %or_and_fusion.2, bf16[448,3,128]{2,0,1:T(8,128)(2,1)S(1)} %get-tuple-element.344, bf16[1792,3,128]{0,2,1:T(8,128)(2,1)S(1)} %bitcast.38), kind=kOutput, calls=%fused_computation.4.clone.1 | convolution fusion | flops 623786688 | bytes 11361280 | tf_op jit(solution)/shard_map/while/body/eval_jaxpr/qhd,khd->hqk/dot_general | solution.py:32
  361.9 5.8 %bitcast_reduce_fusion.2 = f32[3,448]{1,0:T(4,128)S(1)} fusion(f32[3,1792,448]{1,2,0:T(8,128)} %get-tuple-element.306, f32[3,448]{1,0:T(4,128)S(1)} %select_maximum_fusion.2, pred[1792]{0:T(1024)(128)(4,1)S(1)} %or_and_fusion.2), kind=kLoop, calls=%fused_computation.2.clone.1 | loop fusion | flops 9632448 | bytes 9646336 | tf_op jit(solution)/shard_map/while/body/eval_jaxpr/reduce_sum | solution.py:46
  368.6 6.5 %fusion.24 = f32[3,448,128]{2,1,0:T(8,128)} fusion(bf16[1792,3,128]{0,2,1:T(8,128)(2,1)S(1)} %bitcast.39, f32[3,1792,448]{1,2,0:T(8,128)} %get-tuple-element.306, f32[3,448]{1,0:T(4,128)S(1)} %select_maximum_fusion.2, pred[1792]{0:T(1024)(128)(4,1)S(1)} %or_and_fusion.2, f32[3,448,128]{2,1,0:T(8,128)} %get-tuple-element.326, ...), kind=kOutput, calls=%fused_computation.7.clone.1 | convolution fusion | flops 626712576 | bytes 12398849 | tf_op jit(solution)/shard_map/while/body/eval_jaxpr/hqk,khd->hqd/dot_general | solution.py:47
  377.1 3.2 constant_dynamic-slice_fusion.3
  380.3 1.8 copy.34
  382.1 5.3 %select_reduce_fusion.6 = (f32[3,448]{1,0:T(4,128)S(1)}, f32[3,1792,448]{1,2,0:T(8,128)}) fusion(pred[1792]{0:T(1024)(128)(4,1)S(1)} %or_and_fusion.2, bf16[448,3,128]{2,0,1:T(8,128)(2,1)S(1)} %get-tuple-element.344, bf16[1792,3,128]{0,2,1:T(8,128)(2,1)S(1)} %bitcast.38), kind=kOutput, calls=%fused_computation.4.clone.1 | convolution fusion | flops 623786688 | bytes 11361280 | tf_op jit(solution)/shard_map/while/body/eval_jaxpr/qhd,khd->hqk/dot_general | solution.py:32
  387.3 5.8 %bitcast_reduce_fusion.2 = f32[3,448]{1,0:T(4,128)S(1)} fusion(f32[3,1792,448]{1,2,0:T(8,128)} %get-tuple-element.306, f32[3,448]{1,0:T(4,128)S(1)} %select_maximum_fusion.2, pred[1792]{0:T(1024)(128)(4,1)S(1)} %or_and_fusion.2), kind=kLoop, calls=%fused_computation.2.clone.1 | loop fusion | flops 9632448 | bytes 9646336 | tf_op jit(solution)/shard_map/while/body/eval_jaxpr/reduce_sum | solution.py:46
  394.0 6.5 %fusion.24 = f32[3,448,128]{2,1,0:T(8,128)} fusion(bf16[1792,3,128]{0,2,1:T(8,128)(2,1)S(1)} %bitcast.39, f32[3,1792,448]{1,2,0:T(8,128)} %get-tuple-element.306, f32[3,448]{1,0:T(4,128)S(1)} %select_maximum_fusion.2, pred[1792]{0:T(1024)(128)(4,1)S(1)} %or_and_fusion.2, f32[3,448,128]{2,1,0:T(8,128)} %get-tuple-element.326, ...), kind=kOutput, calls=%fused_computation.7.clone.1 | convolution fusion | flops 626712576 | bytes 12398849 | tf_op jit(solution)/shard_map/while/body/eval_jaxpr/hqk,khd->hqd/dot_general | solution.py:47
  400.5 1.4 fusion.9
  402.2 7.8 %convolution_convert_fusion = bf16[448,6144]{1,0:T(8,128)(2,1)} fusion(bf16[448,384]{0,1:T(8,128)(2,1)S(1)} %bitcast.42, bf16[384,6144]{1,0:T(8,128)(2,1)} %param.14), kind=kOutput, calls=%fused_computation.25 | convolution fusion | flops 2116681728 | bytes 10567680 | tf_op jit(solution)/shard_map/dot_general | solution.py:83
  410.7 65.6 %reduce-scatter.2.cloned.1.call-done = bf16[448,768]{1,0:T(8,128)(2,1)} async-done(((bf16[448,6144]{1,0:T(8,128)(2,1)}), bf16[448,768]{1,0:T(8,128)(2,1)}) %reduce-scatter.2.cloned.1.call-update) | async-done | bytes 688144 | tf_op jit(solution)/shard_map/reduce_scatter | solution.py:84
  476.3 1.3 add_convert_fusion
  478.4 20.1 %collective-permute-done = bf16[448,768]{1,0:T(8,128)(2,1)S(1)} collective-permute-done((bf16[448,768]{1,0:T(8,128)(2,1)S(1)}, bf16[448,768]{1,0:T(8,128)(2,1)S(1)}, u32[]{:S(2)}, u32[]{:S(2)}) %collective-permute-start) | collective-permute-done | bytes 688160 | tf_op jit(solution)/shard_map/ppermute | solution.py:14
  (85 shorter events, 22.9 us)
Async XLA Ops:
  6.5 98.2 %all-gather.3.cloned.1.call-start = ((), (), s32[]{:S(2)}) async-start(), calls=%async_computation.1 | async-start | bytes 11354112 | tf_op jit(solution)/shard_map/all_gather | solution.py:61
  7.3 190.4 %all-gather.5.cloned.1.call-start = ((), (), s32[]{:S(2)}) async-start(), calls=%async_computation.2 | async-start | bytes 11354112 | tf_op jit(solution)/shard_map/all_gather | solution.py:62
  8.0 468.3 %reduce-scatter.2.cloned.1.call-start = ((), (), s32[]{:S(2)}) async-start(), calls=%async_computation.3 | async-start | bytes 6193152 | tf_op jit(solution)/shard_map/reduce_scatter | solution.py:84
  400.5 10.1 %copy-start.1 = (f32[64,768]{1,0:T(8,128)S(1)}, f32[64,768]{1,0:T(8,128)}, u32[]{:S(2)}) copy-start(f32[64,768]{1,0:T(8,128)} %param.15) | copy-start | bytes 589828
  400.5 75.8 %copy-start = (bf16[448,768]{1,0:T(8,128)(2,1)S(1)}, bf16[448,768]{1,0:T(8,128)(2,1)}, u32[]{:S(2)}) copy-start(bf16[448,768]{1,0:T(8,128)(2,1)} %param.10) | copy-start | bytes 2064388
  477.7 20.8 %collective-permute-start = (bf16[448,768]{1,0:T(8,128)(2,1)S(1)}, bf16[448,768]{1,0:T(8,128)(2,1)S(1)}, u32[]{:S(2)}, u32[]{:S(2)}) collective-permute-start(bf16[448,768]{1,0:T(8,128)(2,1)S(1)} %add_convert_fusion), channel_id=1, source_target_pairs={{0,248},{8,0},{16,8},{24,16},{32,24},{40,32},{48,40},{56,48},{64,5... | collective-permute-start | bytes 2064392 | tf_op jit(solution)/shard_map/ppermute | solution.py:14
Sparse Core Ops, SparseCore 0:
  9.9 94.8 all-gather.2
  107.3 90.2 all-gather.4
  410.1 66.2 reduce-scatter.1
where the time goes:
time: 507 us; the launch traced here: 506 us
  waiting for transfers between devices  275 us (54%)
  matrix products  102 us (20%)
  other arithmetic  55.6 us (11%)
  local copies, waits for them, and re-layouts  53.5 us (11%)
  between operations  13.8 us (3%)
    all_gather x1, waiting for transfers between devices, per_device(): key_piece = lax.all_gather(key_rows, 'slot', axis=0, tiled=True)  95.3 us
    all_gather x1, waiting for transfers between devices, per_device(): value_piece = lax.all_gather(values, 'slot', axis=0, tiled=True)  92.9 us
    reduce_scatter x1, waiting for transfers between devices, per_device(): lax.psum_scatter(partial_value.astype(jnp.bfloat16), 'tp', scatter_dimens...  65.6 us
    dot_general x8, matrix products, absorb(): jnp.einsum('hqk,khd->hqd', expon.astype(jnp.bfloat16), value_heads, prefe...  52.1 us
    dynamic_slice x32, local copies, waits for them, and re-layouts, per_device(): lax.scan(advance, carry, (key_blocks, value_blocks, jnp.arange(block_tota...  51.1 us
    reduce_sum x8, other arithmetic, absorb(): row_sum = row_sum * shrink + jnp.sum(expon, axis=2)  46.1 us
    dot_general x8, matrix products, absorb(): jnp.einsum('qhd,khd->hqk', query_heads, key_heads, preferred_element_type...  42 us
    ppermute x1, waiting for transfers between devices, passed_along(): return lax.ppermute(value, axis, pairs)  20.1 us
  transfers between devices with their start and end apart: 4, of which 4 were waited for; matrix products, arithmetic and copies ran while one was open for 0% of the time, Pallas kernels for 0%

commit v1 on v0

v1 whole, which is shorter than its diff:
```python
import math

import jax
import jax.numpy as jnp
import numpy as np
from jax import lax
from jax.experimental import pallas as pl
from jax.experimental.pallas import tpu as pltpu
from jax.sharding import Mesh
from jax.sharding import PartitionSpec as P

HD = 128
ROWS = 448
HEADS_HERE = 3
WIDTH = HEADS_HERE * HD
STAT = 32
LOWEST = -1e30
EXP2_SCALE = HD**-0.5 * math.log2(math.e)
Y_STEPS = (0, -1, 1, 2)
SLOT = ("z", "y", "c")
VMEM_LIMIT = 48 * 1024 * 1024


def score(query, key):
    return lax.dot_general(
        query, key, (((1,), (1,)), ((), ())), preferred_element_type=jnp.float32
    )


def attend_kernel(ids, live, *refs):
    query_in, pair_in, out = refs[0:4], refs[4:12], refs[12:16]
    queries, pairs, own, acc, top, done, query_sem, pair_sem, own_sem, out_sem = refs[16:]
    level, y, core = ids[0], ids[1], ids[2]
    first = level * 8
    mine = first + y * 2 + core
    groups = []
    for other in (0, 1):
        for step in Y_STEPS:
            core_there = core if other == 0 else 1 - core
            groups.append(first + lax.rem(y + step + 4, 4) * 2 + core_there)
    alive = [live[first + k] for k in range(8)]

    def live_before(group):
        count = jnp.int32(0)
        for k in range(8):
            count = count + jnp.where(first + k < group, alive[k], 0)
        return count

    n_all = live_before(first + 8)
    n_own = live_before(mine)

    def own_copy():
        return pltpu.make_async_copy(pair_in[0], own, own_sem)

    def query_copy(d):
        return pltpu.make_async_copy(query_in[d], queries.at[d], query_sem.at[d])

    def pair_copy(p):
        place = pl.multiple_of(live_before(groups[p]) * ROWS, 64)
        return pltpu.make_async_copy(pair_in[p], pairs.at[pl.ds(place, ROWS)], pair_sem.at[p])

    own_copy().start()
    for d in range(4):
        query_copy(d).start()
    for p in range(8):

        @pl.when(live[groups[p]] == 1)
        def _():
            pair_copy(p).start()

    for d in range(4):
        query_copy(d).wait()
    own_copy().wait()
    for p in range(8):

        @pl.when(live[groups[p]] == 1)
        def _():
            pair_copy(p).wait()

    def update(d, head, key, value, rows, opening):
        query = queries[d, :, head * HD : (head + 1) * HD]
        scores = score(query, key)
        highest = jnp.max(scores, axis=1, keepdims=True)
        ones = jnp.ones((rows, HD), jnp.bfloat16)
        if opening:
            new = jnp.broadcast_to(highest, (ROWS, HD))
            weights = jnp.exp2(scores * EXP2_SCALE - highest * EXP2_SCALE)
        else:
            old = top[head]
            new = jnp.maximum(old, highest)
            shift = new * EXP2_SCALE
            if rows % HD == 0:
                shift = jnp.concatenate([shift] * (rows // HD), axis=1)
            else:
                shift = shift[:, :1]
            weights = jnp.exp2(scores * EXP2_SCALE - shift)
        weighted = jnp.dot(
            weights.astype(jnp.bfloat16),
            jnp.concatenate([value, ones], axis=1),
            preferred_element_type=jnp.float32,
        )
        if opening:
            acc[head] = weighted
        else:
            shrink = jnp.exp2((old - new) * EXP2_SCALE)
            acc[head] = acc[head] * jnp.concatenate([shrink, shrink], axis=1) + weighted
        top[head] = new

    def update_heads(d, ref, at, rows, opening):
        for head in range(HEADS_HERE):
            low = head * HD
            key = ref[at, low : low + HD]
            value = ref[at, WIDTH + low : WIDTH + low + HD]
            update(d, head, key, value, rows, opening)

    def source(d, unused):
        @pl.when(d == 0)
        def _():
            update_heads(0, own, pl.ds(0, ROWS), ROWS, True)

        @pl.when(d > 0)
        def _():
            top[...] = jnp.full(top.shape, LOWEST, jnp.float32)
            acc[...] = jnp.zeros(acc.shape, jnp.float32)

        count = jnp.where(d == 0, n_own, n_all)

        def two(t, unused_too):
            at = pl.ds(pl.multiple_of(t * 2 * ROWS, HD), 2 * ROWS)
            update_heads(d, pairs, at, 2 * ROWS, False)
            return 0

        lax.fori_loop(0, count // 2, two, 0)

        @pl.when(count % 2 == 1)
        def _():
            at = pl.ds(pl.multiple_of((count - 1) * ROWS, 64), ROWS)
            update_heads(d, pairs, at, ROWS, False)

        lane = lax.broadcasted_iota(jnp.int32, (ROWS, HD), 1)
        stats = jnp.zeros((ROWS, HD), jnp.float32)
        for head in range(HEADS_HERE):
            exact = top[head]
            sent = exact.astype(jnp.bfloat16).astype(jnp.float32)
            factor = jnp.exp2((exact - sent) * EXP2_SCALE)
            both = acc[head]
            done[d, 0:ROWS, head * HD : (head + 1) * HD] = (both[:, :HD] * factor).astype(
                jnp.bfloat16
            )
            total = both[:, HD:] * factor
            high = total.astype(jnp.bfloat16).astype(jnp.float32)
            stats = jnp.where(lane == head, sent, stats)
            stats = jnp.where(lane == HEADS_HERE + head, high, stats)
            stats = jnp.where(lane == 2 * HEADS_HERE + head, total - high, stats)
        flat = jnp.transpose(stats)[:16].astype(jnp.bfloat16)
        done[d, ROWS : ROWS + 16, :] = flat[:, :WIDTH]
        rest = jnp.zeros((16, 2 * WIDTH - ROWS), jnp.bfloat16)
        done[d, ROWS + 16 : ROWS + 32, :] = jnp.concatenate([flat[:, WIDTH:], rest], axis=1)
        return 0

    lax.fori_loop(0, 4 - level, source, 0)
    for d in range(4):
        pltpu.make_async_copy(done.at[d], out[d], out_sem.at[d]).start()
    for d in range(4):
        pltpu.make_async_copy(done.at[d], out[d], out_sem.at[d]).wait()


def attend(ids, live, queries, pairs):
    smem = pl.BlockSpec(memory_space=pltpu.SMEM)
    anywhere = pl.BlockSpec(memory_space=pl.ANY)
    bf16, f32 = jnp.bfloat16, jnp.float32
    return pl.pallas_call(
        attend_kernel,
        out_shape=[jax.ShapeDtypeStruct((ROWS + STAT, WIDTH), bf16)] * 4,
        in_specs=[smem, smem] + [anywhere] * 12,
        out_specs=[anywhere] * 4,
        scratch_shapes=[
            pltpu.VMEM((4, ROWS, WIDTH), bf16),
            pltpu.VMEM((8 * ROWS, 2 * WIDTH), bf16),
            pltpu.VMEM((ROWS, 2 * WIDTH), bf16),
            pltpu.VMEM((HEADS_HERE, ROWS, 2 * HD), f32),
            pltpu.VMEM((HEADS_HERE, ROWS, HD), f32),
            pltpu.VMEM((4, ROWS + STAT, WIDTH), bf16),
            pltpu.SemaphoreType.DMA((4,)),
            pltpu.SemaphoreType.DMA((8,)),
            pltpu.SemaphoreType.DMA,
            pltpu.SemaphoreType.DMA((4,)),
        ],
        compiler_params=pltpu.CompilerParams(vmem_limit_bytes=VMEM_LIMIT),
        name="attend",
    )(ids, live, *queries, *pairs)


def combine_kernel(ids, *refs):
    parts, out = refs[0:4], refs[4]
    home = ids[3]
    maxima, sums = [], []
    for d in range(4):
        tail = parts[d][ROWS : ROWS + STAT, :].astype(jnp.float32)
        flat = jnp.concatenate([tail[0:16], tail[16:32, : ROWS - WIDTH]], axis=1)
        stats = jnp.transpose(jnp.concatenate([flat, jnp.zeros((HD - 16, ROWS), jnp.float32)]))
        present = d <= home
        row_max, row_sum = [], []
        for head in range(HEADS_HERE):
            total = (
                stats[:, HEADS_HERE + head : HEADS_HERE + head + 1]
                + stats[:, 2 * HEADS_HERE + head : 2 * HEADS_HERE + head + 1]
            )
            row_max.append(jnp.where(present, stats[:, head : head + 1], LOWEST))
            row_sum.append(total)
        maxima.append(row_max)
        sums.append(row_sum)
    for head in range(HEADS_HERE):
        at = slice(head * HD, (head + 1) * HD)
        highest = maxima[0][head]
        for d in range(1, 4):
            highest = jnp.maximum(highest, maxima[d][head])
        numerator = jnp.zeros((ROWS, HD), jnp.float32)
        denominator = jnp.zeros((ROWS, 1), jnp.float32)
        for d in range(4):
            factor = jnp.exp2((maxima[d][head] - highest) * EXP2_SCALE)
            numerator = numerator + parts[d][0:ROWS, at].astype(jnp.float32) * factor
            denominator = denominator + sums[d][head] * factor
        out[:, at] = (numerator / denominator).astype(jnp.bfloat16)


def combine(ids, parts):
    vmem = pl.BlockSpec(memory_space=pltpu.VMEM)
    return pl.pallas_call(
        combine_kernel,
        out_shape=jax.ShapeDtypeStruct((ROWS, WIDTH), jnp.bfloat16),
        in_specs=[pl.BlockSpec(memory_space=pltpu.SMEM)] + [vmem] * 4,
        out_specs=vmem,
        compiler_params=pltpu.CompilerParams(vmem_limit_bytes=VMEM_LIMIT),
        name="combine",
    )(ids, *parts)


def around(value, axis, steps):
    count = lax.axis_size(axis)
    return lax.ppermute(value, axis, [(i, (i + steps) % count) for i in range(count)])


def per_device(hidden, queries, key_rows, values, out_weight, level_table, noise_level, group_live):
    z, y, core = lax.axis_index("z"), lax.axis_index("y"), lax.axis_index("c")
    w, x = lax.axis_index("w"), lax.axis_index("x")
    slot = z * 8 + y * 2 + core
    home = lax.rem(slot + 1, 32) // 8
    ids = jnp.stack([z, y, core, home]).astype(jnp.int32)

    pair = jnp.concatenate([key_rows, values], axis=1)
    pairs = [pair] + [around(pair, "y", -step) for step in Y_STEPS[1:]]
    pairs = pairs + [around(p, "c", 1) for p in pairs]
    sources = [queries] + [
        lax.ppermute(queries, "z", [(i, i - d) for i in range(d, 4)]) for d in (1, 2, 3)
    ]

    part = out_weight.shape[1] // 8
    pieces = []
    for step in range(4):
        there = lax.rem(x + step, 4)
        near = lax.dynamic_slice_in_dim(out_weight, (w * 4 + there) * part, part, 1)
        far = lax.dynamic_slice_in_dim(out_weight, ((1 - w) * 4 + there) * part, part, 1)
        piece = jnp.concatenate([near, far], axis=1)
        pieces.append(piece if step == 0 else around(piece, "x", step))
    weight = jnp.concatenate(pieces, axis=0)

    hidden_next = around(hidden, SLOT, -1)
    level_next = around(noise_level, SLOT, -1)

    shares = attend(ids, group_live, sources, pairs)
    back = []
    for d in range(4):
        pairs_back = [
            (8 * (i - d) + j, (8 * i + j - 1) % 32) for i in range(d, 4) for j in range(8)
        ]
        back.append(lax.ppermute(shares[d], SLOT, pairs_back))
    attended = combine(ids, back)

    gathered = [attended] + [around(attended, "x", step) for step in (1, 2, 3)]
    rows = jnp.concatenate(gathered, axis=1)
    far_sum = jnp.dot(rows, weight[:, part:], preferred_element_type=jnp.float32)
    arrived = around(far_sum.astype(jnp.bfloat16), "w", 1)
    near_sum = jnp.dot(rows, weight[:, :part], preferred_element_type=jnp.float32)
    projected = near_sum + arrived.astype(jnp.float32)
    gate_row = lax.dynamic_slice_in_dim(level_table, level_next[0], 1, 0)
    return (hidden_next.astype(jnp.float32) + gate_row * projected).astype(jnp.bfloat16)


def solution(mesh):
    fine = Mesh(np.asarray(mesh.devices).reshape(4, 4, 2, 2, 4), ("z", "y", "c", "w", "x"))
    tp = ("w", "x")
    block = P(SLOT, tp)
    in_specs = (block, block, block, block, P(tp, None), P(None, tp), P(SLOT), P())
    return jax.shard_map(
        per_device, mesh=fine, in_specs=in_specs, out_specs=block, check_vma=False
    )
```

time: 507 us -> 178 us (0.35)
  the two profiles are of different devices: /device:TPU:25 before, /device:TPU:1 now
where the time goes in v1:
time: 178 us; the launch traced here: 177 us
  waiting for transfers between devices  69.2 us (39%)
  starting transfers between devices  50.8 us (29%)
  Pallas kernels  30.9 us (17%)
  other arithmetic  9.03 us (5%)
  local copies, waits for them, and re-layouts  8.44 us (5%)
  matrix products  6.14 us (3%)
  between operations  2.15 us (1%)
    ppermute x16, starting transfers between devices, around(): lax.ppermute(value, axis, [(i, (i + steps) % count) for i in range(count)])  30.3 us
    pallas_call x1, Pallas kernels, attend(): pl.pallas_call(attend_kernel, out_shape=[jax.ShapeDtypeStruct((ROWS + STA...  28.7 us
    ppermute x16, waiting for transfers between devices, around(): lax.ppermute(value, axis, [(i, (i + steps) % count) for i in range(count)])  25.8 us
    ppermute x3, waiting for transfers between devices, per_device(): lax.ppermute(queries, 'z', [(i, i - d) for i in range(d, 4)])  24.5 us
    ppermute x4, waiting for transfers between devices, per_device(): back.append(lax.ppermute(shares[d], SLOT, pairs_back))  18.9 us
    ppermute x4, starting transfers between devices, per_device(): back.append(lax.ppermute(shares[d], SLOT, pairs_back))  16.6 us
    concatenate x1, other arithmetic, per_device(): weight = jnp.concatenate(pieces, axis=0)  5.61 us
    dot_general x1, matrix products, per_device(): jnp.dot(rows, weight[:, :part], preferred_element_type=jnp.float32)  3.92 us
  transfers between devices with their start and end apart: 23, of which 11 were waited for; matrix products, arithmetic and copies ran while one was open for 8% of the time, Pallas kernels for 17%

profile of v1, /device:TPU:1, one launch (start us, length us, event | category | flops | bytes accessed | tf_op | source)
XLA Modules:
  0.0 176.7 jit_solution(17893323615959317681)
XLA Ops:
  0.0 1.1 constant_dynamic-update-slice_fusion.1
  1.1 1.0 constant_dynamic-update-slice_fusion.refs_4_
  2.1 3.6 %collective-permute-start.6 = (bf16[448,768]{1,0:T(8,128)(2,1)S(1)}, bf16[448,768]{1,0:T(8,128)(2,1)S(1)}, u32[]{:S(2)}, u32[]{:S(2)}) collective-permute-start(bf16[448,768]{1,0:T(8,128)(2,1)S(1)} %constant_dynamic-update-slice_fusion.refs_4_), channel_id=1, source_target_pairs={{0,48},{16,0},{32,16},{48,32},{1,49},{17,1},{33,17},{49,33},{2,50}... | collective-permute-start | bytes 2064392 | tf_op jit(solution)/shard_map/ppermute | solution.py:241
  5.7 1.3 collective-permute-start.2
  7.0 0.4 collective-permute-start.7
  7.5 0.7 collective-permute-start.5
  8.2 1.3 collective-permute-start.3
  9.5 3.7 %constant_dynamic-slice_fusion.7 = (bf16[384,768]{1,0:T(8,128)(2,1)}, bf16[384,768]{1,0:T(8,128)(2,1)S(1)}, bf16[384,768]{1,0:T(8,128)(2,1)S(1)}, bf16[384,768]{...) fusion(bf16[384,6144]{1,0:T(8,128)(2,1)} %param.12, ...), kind=kLoop, calls=%fused_computation.21 | loop fusion | bytes 9437216 | tf_op jit(solution)/shard_map/dynamic_slice | solution.py:262
  13.2 13.8 %collective-permute-done.2.refs_1_ = bf16[448,384]{1,0:T(8,128)(2,1)} collective-permute-done((bf16[448,384]{1,0:T(8,128)(2,1)}, bf16[448,384]{1,0:T(8,128)(2,1)}, u32[]{:S(2)}, u32[]{:S(2)}) %collective-permute-start.2) | collective-permute-done | bytes 344096 | tf_op jit(solution)/shard_map/ppermute | solution.py:255
  27.0 1.7 collective-permute-start.8
  28.7 5.7 %collective-permute-done.6.refs_6_ = bf16[448,768]{1,0:T(8,128)(2,1)S(1)} collective-permute-done((bf16[448,768]{1,0:T(8,128)(2,1)S(1)}, bf16[448,768]{1,0:T(8,128)(2,1)S(1)}, u32[]{:S(2)}, u32[]{:S(2)}) %collective-permute-start.6) | collective-permute-done | bytes 688160 | tf_op jit(solution)/shard_map/ppermute | solution.py:241
  34.4 1.7 collective-permute-start.10
  36.1 1.1 pad_maximum_fusion.2
  37.3 1.3 collective-permute-start.4
  38.5 0.0 copy-start.4
  38.6 1.1 pad_maximum_fusion.3
  39.7 0.0 collective-permute-start.11
  39.7 1.1 collective-permute-done.5.refs_5_
  40.7 0.5 collective-permute-start.9
  41.2 1.1 pad_maximum_fusion.4
  42.3 10.7 %collective-permute-done.4.refs_3_ = bf16[448,384]{1,0:T(8,128)(2,1)S(1)} collective-permute-done((bf16[448,384]{1,0:T(8,128)(2,1)S(1)}, bf16[448,384]{1,0:T(8,128)(2,1)S(1)}, u32[]{:S(2)}, u32[]{:S(2)}) %collective-permute-start.4) | collective-permute-done | bytes 344096 | tf_op jit(solution)/shard_map/ppermute | solution.py:255
  53.0 0.7 copy-done.2
  53.8 1.2 collective-permute-start.19
  55.0 2.5 %collective-permute-start.20 = (bf16[384,1536]{1,0:T(8,128)(2,1)}, bf16[384,1536]{1,0:T(8,128)(2,1)}, u32[]{:S(2)}, u32[]{:S(2)}) collective-permute-start(bf16[384,1536]{1,0:T(8,128)(2,1)} %pad_maximum_fusion.3), channel_id=1, source_target_pairs={{0,2},{1,3},{2,0},{3,1},{4,6},{5,7},{6,4},{7,5},{8,10},{9,11},{10,... | collective-permute-start | bytes 3538952 | tf_op jit(solution)/shard_map/ppermute | solution.py:241
  57.4 0.9 copy-done.9
  58.3 1.2 collective-permute-start.21
  59.5 0.1 pad_add_fusion.ids
  59.6 1.0 copy-done.3
  60.6 28.7 %attend.1 = (bf16[480,384]{1,0:T(8,128)(2,1)S(1)}, bf16[480,384]{1,0:T(8,128)(2,1)S(1)}, bf16[480,384]{1,0:T(8,128)(2,1)S(1)}, bf16[480,384]{1,0:T(8,128)(2,1)S(1)}) custom-call(s32[4]{0:T(128)S(1)} %pad_add_fusion.ids, s32[32]{0:T(128)S(1)} %copy-done.4, bf16[448,384]{1,0:T(8,128)(2,1)S(1)} %copy-done.1, bf16[448,384]{1,0:T(8,128)(2,1)} %collective-permute-done.2.refs_1_, ...), custom_call_target="tpu_custom_call" | custom-call | tf_op jit(solution)/shard_map/attend/pallas_call | solution.py:172
  89.2 1.6 collective-permute-start.12
  90.8 12.5 %collective-permute-start.13 = (bf16[480,384]{1,0:T(8,128)(2,1)S(1)}, bf16[480,384]{1,0:T(8,128)(2,1)S(1)}, u32[]{:S(2)}, u32[]{:S(2)}) collective-permute-start(bf16[480,384]{1,0:T(8,128)(2,1)S(1)} %get-tuple-element.10), channel_id=1, source_target_pairs={{0,56},{8,64},{16,72},{24,80},{32,88},{40,96},{48,104},{56,112},{6... | collective-permute-start | bytes 1105928 | tf_op jit(solution)/shard_map/ppermute | solution.py:277
  103.3 1.3 collective-permute-start.14
  104.6 6.6 %collective-permute-done.13.refs_1_ = bf16[480,384]{1,0:T(8,128)(2,1)S(1)} collective-permute-done((bf16[480,384]{1,0:T(8,128)(2,1)S(1)}, bf16[480,384]{1,0:T(8,128)(2,1)S(1)}, u32[]{:S(2)}, u32[]{:S(2)}) %collective-permute-start.13) | collective-permute-done | bytes 368672 | tf_op jit(solution)/shard_map/ppermute | solution.py:277
  111.2 1.3 collective-permute-start.15
  112.5 5.6 %collective-permute-done.14.refs_2_ = bf16[480,384]{1,0:T(8,128)(2,1)S(1)} collective-permute-done((bf16[480,384]{1,0:T(8,128)(2,1)S(1)}, bf16[480,384]{1,0:T(8,128)(2,1)S(1)}, u32[]{:S(2)}, u32[]{:S(2)}) %collective-permute-start.14) | collective-permute-done | bytes 368672 | tf_op jit(solution)/shard_map/ppermute | solution.py:277
  118.1 6.8 %collective-permute-done.15.refs_3_ = bf16[480,384]{1,0:T(8,128)(2,1)S(1)} collective-permute-done((bf16[480,384]{1,0:T(8,128)(2,1)S(1)}, bf16[480,384]{1,0:T(8,128)(2,1)S(1)}, u32[]{:S(2)}, u32[]{:S(2)}) %collective-permute-start.15) | collective-permute-done | bytes 368672 | tf_op jit(solution)/shard_map/ppermute | solution.py:277
  124.9 2.2 %combine.1 = bf16[448,384]{1,0:T(8,128)(2,1)S(1)} custom-call(s32[4]{0:T(128)S(1)} %pad_add_fusion.ids, bf16[480,384]{1,0:T(8,128)(2,1)S(1)} %collective-permute-done.12.refs_0_, bf16[480,384]{1,0:T(8,128)(2,1)S(1)} %collective-permute-done.13.refs_1_, bf16[480,384]{1,0:T(8,128)(2,1)S(1)} %collective-permute-done.14.refs_2_, ...), custom_call_target="tpu_custom_call" | custom-call | tf_op jit(solution)/shard_map/combine/pallas_call | solution.py:229
  127.1 0.4 collective-permute-start.16
  127.5 0.9 collective-permute-start.17
  128.4 1.8 %collective-permute-start.18 = (bf16[448,384]{1,0:T(8,128)(2,1)S(1)}, bf16[448,384]{1,0:T(8,128)(2,1)}, u32[]{:S(2)}, u32[]{:S(2)}) collective-permute-start(bf16[448,384]{1,0:T(8,128)(2,1)S(1)} %combine.1), channel_id=1, source_target_pairs={{0,3},{1,0},{2,1},{3,2},{4,7},{5,4},{6,5},{7,6},{8,11},{9,8},{10,9... | collective-permute-start | bytes 1032200 | tf_op jit(solution)/shard_map/ppermute | solution.py:241
  130.2 5.6 %pad_maximum_fusion = bf16[1536,1536]{1,0:T(8,128)(2,1)S(1)} fusion(bf16[384,1536]{1,0:T(8,128)(2,1)} %collective-permute-done.21, bf16[384,1536]{1,0:T(8,128)(2,1)} %collective-permute-done.20, bf16[384,1536]{1,0:T(8,128)(2,1)} %collective-permute-done.19, bf16[384,768]{1,0:T(8,128)(2,1)S(1)} %copy-done.7, bf16[384,768]{1,0:T(8,128)(2,1)S(1)} %copy-done.6), kind=kLoop, calls=%fused_computation | loop fusion | flops 23592960 | bytes 9437184 | tf_op jit(solution)/shard_map/concatenate | solution.py:266
  135.8 4.9 %collective-permute-done.16 = bf16[448,384]{1,0:T(8,128)(2,1)S(1)} collective-permute-done((bf16[448,384]{1,0:T(8,128)(2,1)S(1)}, bf16[448,384]{1,0:T(8,128)(2,1)S(1)}, u32[]{:S(2)}, u32[]{:S(2)}) %collective-permute-start.16) | collective-permute-done | bytes 344096 | tf_op jit(solution)/shard_map/ppermute | solution.py:241
  140.7 1.0 collective-permute-done.18
  141.7 2.2 %fusion.4 = bf16[448,768]{1,0:T(8,128)(2,1)S(1)} fusion(bf16[1536,1536]{1,0:T(8,128)(2,1)S(1)} %pad_maximum_fusion, bf16[448,384]{1,0:T(8,128)(2,1)} %collective-permute-done.18, bf16[448,384]{1,0:T(8,128)(2,1)S(1)} %collective-permute-done.17, bf16[448,384]{1,0:T(8,128)(2,1)S(1)} %collective-permute-done.16, bf16[448,384]{1,0:T(8,128)(2,1)S(1)} %combine.1), kind=kOutput, calls=%fused_computation.7 | convolution fusion | flops 1062813696 | bytes 4423680 | tf_op jit(solution)/shard_map/dot_general | solution.py:282
  144.0 13.8 %collective-permute-start.22 = (bf16[448,768]{1,0:T(8,128)(2,1)S(1)}, bf16[448,768]{1,0:T(8,128)(2,1)S(1)}, u32[]{:S(2)}, u32[]{:S(2)}) collective-permute-start(bf16[448,768]{1,0:T(8,128)(2,1)S(1)} %fusion.4), channel_id=1, source_target_pairs={{0,4},{4,0},{1,5},{5,1},{2,6},{6,2},{3,7},{7,3},{8,12},{12,8},{9,1... | collective-permute-start | bytes 2064392 | tf_op jit(solution)/shard_map/ppermute | solution.py:241
  157.7 3.4 %collective-permute-done.1 = s32[1]{0:T(128)} collective-permute-done((s32[1]{0:T(128)}, s32[1]{0:T(128)}, u32[]{:S(2)}, u32[]{:S(2)}) %collective-permute-start.1) | collective-permute-done | bytes 36 | tf_op jit(solution)/shard_map/ppermute | solution.py:241
  163.1 9.7 %collective-permute-done.22 = bf16[448,768]{1,0:T(8,128)(2,1)S(1)} collective-permute-done((bf16[448,768]{1,0:T(8,128)(2,1)S(1)}, bf16[448,768]{1,0:T(8,128)(2,1)S(1)}, u32[]{:S(2)}, u32[]{:S(2)}) %collective-permute-start.22) | collective-permute-done | bytes 688160 | tf_op jit(solution)/shard_map/ppermute | solution.py:241
  172.8 3.9 %add_convert_fusion = bf16[448,768]{1,0:T(8,128)(2,1)} fusion(bf16[448,768]{1,0:T(8,128)(2,1)S(1)} %collective-permute-done.22, bf16[448,768]{1,0:T(8,128)(2,1)S(1)} %collective-permute-done, f32[768]{0:T(1024)S(1)} %dynamic-slice_reduce_fusion, bf16[1536,1536]{1,0:T(8,128)(2,1)} %copy-done.5, bf16[448,384]{1,0:T(8,128)(2,1)} %collective-permute-done.18, ...), kind=kOutput, calls=%fused_computation.6 | convolution fusion | flops 1064534016 | bytes 5803008 | tf_op jit(solution)/shard_map/dot_general | solution.py:284
  (31 shorter events, 0.1 us)
Async XLA Ops:
  0.0 163.0 %copy-start = (f32[64,768]{1,0:T(8,128)S(1)}, f32[64,768]{1,0:T(8,128)}, u32[]{:S(2)}) copy-start(f32[64,768]{1,0:T(8,128)} %param.13) | copy-start | bytes 589828
  2.1 32.3 %collective-permute-start.6 = (bf16[448,768]{1,0:T(8,128)(2,1)S(1)}, bf16[448,768]{1,0:T(8,128)(2,1)S(1)}, u32[]{:S(2)}, u32[]{:S(2)}) collective-permute-start(bf16[448,768]{1,0:T(8,128)(2,1)S(1)} %constant_dynamic-update-slice_fusion.refs_4_), channel_id=1, source_target_pairs={{0,48},{16,0},{32,16},{48,32},{1,49},{17,1},{33,17},{49,33},{2,50}... | collective-permute-start | bytes 2064392 | tf_op jit(solution)/shard_map/ppermute | solution.py:241
  5.7 21.3 %collective-permute-start.2 = (bf16[448,384]{1,0:T(8,128)(2,1)}, bf16[448,384]{1,0:T(8,128)(2,1)}, u32[]{:S(2)}, u32[]{:S(2)}) collective-permute-start(bf16[448,384]{1,0:T(8,128)(2,1)} %refs_0_.1), channel_id=1, source_target_pairs={{64,0},{128,64},{192,128},{65,1},{129,65},{193,129},{66,2},{130,66... | collective-permute-start | bytes 1032200 | tf_op jit(solution)/shard_map/ppermute | solution.py:255
  7.0 32.6 %collective-permute-start.7 = (bf16[448,768]{1,0:T(8,128)(2,1)S(1)}, bf16[448,768]{1,0:T(8,128)(2,1)S(1)}, u32[]{:S(2)}, u32[]{:S(2)}) collective-permute-start(bf16[448,768]{1,0:T(8,128)(2,1)S(1)} %constant_dynamic-update-slice_fusion.refs_4_), channel_id=1, source_target_pairs={{0,32},{16,48},{32,0},{48,16},{1,33},{17,49},{33,1},{49,17},{2,34}... | collective-permute-start | bytes 2064392 | tf_op jit(solution)/shard_map/ppermute | solution.py:241
  7.5 33.3 %collective-permute-start.5 = (bf16[448,768]{1,0:T(8,128)(2,1)S(1)}, bf16[448,768]{1,0:T(8,128)(2,1)S(1)}, u32[]{:S(2)}, u32[]{:S(2)}) collective-permute-start(bf16[448,768]{1,0:T(8,128)(2,1)S(1)} %constant_dynamic-update-slice_fusion.refs_4_), channel_id=1, source_target_pairs={{0,16},{16,32},{32,48},{48,0},{1,17},{17,33},{33,49},{49,1},{2,18}... | collective-permute-start | bytes 2064392 | tf_op jit(solution)/shard_map/ppermute | solution.py:241
  8.2 29.1 %collective-permute-start.3 = (bf16[448,384]{1,0:T(8,128)(2,1)}, bf16[448,384]{1,0:T(8,128)(2,1)}, u32[]{:S(2)}, u32[]{:S(2)}) collective-permute-start(bf16[448,384]{1,0:T(8,128)(2,1)} %refs_0_.1), channel_id=1, source_target_pairs={{128,0},{192,64},{129,1},{193,65},{130,2},{194,66},{131,3},{195,67... | collective-permute-start | bytes 1032200 | tf_op jit(solution)/shard_map/ppermute | solution.py:255
  13.2 24.1 %copy-start.1 = (bf16[448,384]{1,0:T(8,128)(2,1)S(1)}, bf16[448,384]{1,0:T(8,128)(2,1)}, u32[]{:S(2)}) copy-start(bf16[448,384]{1,0:T(8,128)(2,1)} %refs_0_.1) | copy-start | bytes 1032196
  27.0 28.0 %collective-permute-start.8 = (bf16[448,768]{1,0:T(8,128)(2,1)S(1)}, bf16[448,768]{1,0:T(8,128)(2,1)S(1)}, u32[]{:S(2)}, u32[]{:S(2)}) collective-permute-start(bf16[448,768]{1,0:T(8,128)(2,1)S(1)} %constant_dynamic-update-slice_fusion.refs_4_), channel_id=1, source_target_pairs={{0,8},{8,0},{1,9},{9,1},{2,10},{10,2},{3,11},{11,3},{4,12},{12,4},... | collective-permute-start | bytes 2064392 | tf_op jit(solution)/shard_map/ppermute | solution.py:241
  34.4 23.0 %collective-permute-start.10 = (bf16[448,768]{1,0:T(8,128)(2,1)S(1)}, bf16[448,768]{1,0:T(8,128)(2,1)S(1)}, u32[]{:S(2)}, u32[]{:S(2)}) collective-permute-start(bf16[448,768]{1,0:T(8,128)(2,1)S(1)} %collective-permute-done.6.refs_6_), channel_id=1, source_target_pairs={{0,8},{8,0},{1,9},{9,1},{2,10},{10,2},{3,11},{11,3},{4,12},{12,4},... | collective-permute-start | bytes 2064392 | tf_op jit(solution)/shard_map/ppermute | solution.py:241
  37.3 15.8 %collective-permute-start.4 = (bf16[448,384]{1,0:T(8,128)(2,1)S(1)}, bf16[448,384]{1,0:T(8,128)(2,1)S(1)}, u32[]{:S(2)}, u32[]{:S(2)}) collective-permute-start(bf16[448,384]{1,0:T(8,128)(2,1)S(1)} %copy-done.1), channel_id=1, source_target_pairs={{192,0},{193,1},{194,2},{195,3},{196,4},{197,5},{198,6},{199,7},{2... | collective-permute-start | bytes 1032200 | tf_op jit(solution)/shard_map/ppermute | solution.py:255
  38.5 21.0 %copy-start.4 = (s32[32]{0:T(128)S(1)}, s32[32]{0:T(128)}, u32[]{:S(2)}) copy-start(s32[32]{0:T(128)} %live.1) | copy-start | bytes 388
  39.7 19.9 %collective-permute-start.11 = (bf16[448,768]{1,0:T(8,128)(2,1)S(1)}, bf16[448,768]{1,0:T(8,128)(2,1)}, u32[]{:S(2)}, u32[]{:S(2)}) collective-permute-start(bf16[448,768]{1,0:T(8,128)(2,1)S(1)} %collective-permute-done.7.refs_7_), channel_id=1, source_target_pairs={{0,8},{8,0},{1,9},{9,1},{2,10},{10,2},{3,11},{11,3},{4,12},{12,4},... | collective-permute-start | bytes 2064392 | tf_op jit(solution)/shard_map/ppermute | solution.py:241
  40.7 18.9 %collective-permute-start.9 = (bf16[448,768]{1,0:T(8,128)(2,1)S(1)}, bf16[448,768]{1,0:T(8,128)(2,1)}, u32[]{:S(2)}, u32[]{:S(2)}) collective-permute-start(bf16[448,768]{1,0:T(8,128)(2,1)S(1)} %collective-permute-done.5.refs_5_), channel_id=1, source_target_pairs={{0,8},{8,0},{1,9},{9,1},{2,10},{10,2},{3,11},{11,3},{4,12},{12,4},... | collective-permute-start | bytes 2064392 | tf_op jit(solution)/shard_map/ppermute | solution.py:241
  53.0 0.7 copy-start.2
  53.8 73.8 %collective-permute-start.19 = (bf16[384,1536]{1,0:T(8,128)(2,1)}, bf16[384,1536]{1,0:T(8,128)(2,1)}, u32[]{:S(2)}, u32[]{:S(2)}) collective-permute-start(bf16[384,1536]{1,0:T(8,128)(2,1)} %pad_maximum_fusion.2), channel_id=1, source_target_pairs={{0,1},{1,2},{2,3},{3,0},{4,5},{5,6},{6,7},{7,4},{8,9},{9,10},{10,1... | collective-permute-start | bytes 3538952 | tf_op jit(solution)/shard_map/ppermute | solution.py:241
  55.0 2.5 %copy-start.8 = (bf16[448,768]{1,0:T(8,128)(2,1)}, bf16[448,768]{1,0:T(8,128)(2,1)S(1)}, u32[]{:S(2)}) copy-start(bf16[448,768]{1,0:T(8,128)(2,1)S(1)} %collective-permute-done.8.refs_8_) | copy-start | bytes 2064388
  55.0 73.4 %collective-permute-start.20 = (bf16[384,1536]{1,0:T(8,128)(2,1)}, bf16[384,1536]{1,0:T(8,128)(2,1)}, u32[]{:S(2)}, u32[]{:S(2)}) collective-permute-start(bf16[384,1536]{1,0:T(8,128)(2,1)} %pad_maximum_fusion.3), channel_id=1, source_target_pairs={{0,2},{1,3},{2,0},{3,1},{4,6},{5,7},{6,4},{7,5},{8,10},{9,11},{10,... | collective-permute-start | bytes 3538952 | tf_op jit(solution)/shard_map/ppermute | solution.py:241
  57.4 0.9 copy-start.9
  58.3 71.9 %collective-permute-start.21 = (bf16[384,1536]{1,0:T(8,128)(2,1)}, bf16[384,1536]{1,0:T(8,128)(2,1)}, u32[]{:S(2)}, u32[]{:S(2)}) collective-permute-start(bf16[384,1536]{1,0:T(8,128)(2,1)} %pad_maximum_fusion.4), channel_id=1, source_target_pairs={{0,3},{1,0},{2,1},{3,2},{4,7},{5,4},{6,5},{7,6},{8,11},{9,8},{10,9... | collective-permute-start | bytes 3538952 | tf_op jit(solution)/shard_map/ppermute | solution.py:241
  59.6 1.0 copy-start.3
  60.6 69.6 %copy-start.6 = (bf16[384,768]{1,0:T(8,128)(2,1)S(1)}, bf16[384,768]{1,0:T(8,128)(2,1)}, u32[]{:S(2)}) copy-start(bf16[384,768]{1,0:T(8,128)(2,1)} %get-tuple-element.13) | copy-start | bytes 1769476
  60.6 69.6 %copy-start.7 = (bf16[384,768]{1,0:T(8,128)(2,1)S(1)}, bf16[384,768]{1,0:T(8,128)(2,1)}, u32[]{:S(2)}) copy-start(bf16[384,768]{1,0:T(8,128)(2,1)} %get-tuple-element.18) | copy-start | bytes 1769476
  89.2 14.0 %collective-permute-start.12 = (bf16[480,384]{1,0:T(8,128)(2,1)S(1)}, bf16[480,384]{1,0:T(8,128)(2,1)S(1)}, u32[]{:S(2)}, u32[]{:S(2)}) collective-permute-start(bf16[480,384]{1,0:T(8,128)(2,1)S(1)} %get-tuple-element.9), channel_id=1, source_target_pairs={{0,248},{8,0},{16,8},{24,16},{32,24},{40,32},{48,40},{56,48},{64,5... | collective-permute-start | bytes 1105928 | tf_op jit(solution)/shard_map/ppermute | solution.py:277
  90.8 20.4 %collective-permute-start.13 = (bf16[480,384]{1,0:T(8,128)(2,1)S(1)}, bf16[480,384]{1,0:T(8,128)(2,1)S(1)}, u32[]{:S(2)}, u32[]{:S(2)}) collective-permute-start(bf16[480,384]{1,0:T(8,128)(2,1)S(1)} %get-tuple-element.10), channel_id=1, source_target_pairs={{0,56},{8,64},{16,72},{24,80},{32,88},{40,96},{48,104},{56,112},{6... | collective-permute-start | bytes 1105928 | tf_op jit(solution)/shard_map/ppermute | solution.py:277
  103.3 14.8 %collective-permute-start.14 = (bf16[480,384]{1,0:T(8,128)(2,1)S(1)}, bf16[480,384]{1,0:T(8,128)(2,1)S(1)}, u32[]{:S(2)}, u32[]{:S(2)}) collective-permute-start(bf16[480,384]{1,0:T(8,128)(2,1)S(1)} %get-tuple-element.11), channel_id=1, source_target_pairs={{0,120},{8,128},{16,136},{24,144},{32,152},{40,160},{48,168},{56,1... | collective-permute-start | bytes 1105928 | tf_op jit(solution)/shard_map/ppermute | solution.py:277
  111.2 13.6 %collective-permute-start.15 = (bf16[480,384]{1,0:T(8,128)(2,1)S(1)}, bf16[480,384]{1,0:T(8,128)(2,1)S(1)}, u32[]{:S(2)}, u32[]{:S(2)}) collective-permute-start(bf16[480,384]{1,0:T(8,128)(2,1)S(1)} %get-tuple-element.12), channel_id=1, source_target_pairs={{0,184},{8,192},{16,200},{24,208},{32,216},{40,224},{48,232},{56,2... | collective-permute-start | bytes 1105928 | tf_op jit(solution)/shard_map/ppermute | solution.py:277
  118.1 45.0 %collective-permute-start = (bf16[448,768]{1,0:T(8,128)(2,1)}, bf16[448,768]{1,0:T(8,128)(2,1)S(1)}, u32[]{:S(2)}, u32[]{:S(2)}) collective-permute-start(bf16[448,768]{1,0:T(8,128)(2,1)} %param.8), channel_id=1, source_target_pairs={{0,248},{8,0},{16,8},{24,16},{32,24},{40,32},{48,40},{56,48},{64,5... | collective-permute-start | bytes 2064392 | tf_op jit(solution)/shard_map/ppermute | solution.py:241
  127.1 13.6 %collective-permute-start.16 = (bf16[448,384]{1,0:T(8,128)(2,1)S(1)}, bf16[448,384]{1,0:T(8,128)(2,1)S(1)}, u32[]{:S(2)}, u32[]{:S(2)}) collective-permute-start(bf16[448,384]{1,0:T(8,128)(2,1)S(1)} %combine.1), channel_id=1, source_target_pairs={{0,1},{1,2},{2,3},{3,0},{4,5},{5,6},{6,7},{7,4},{8,9},{9,10},{10,1... | collective-permute-start | bytes 1032200 | tf_op jit(solution)/shard_map/ppermute | solution.py:241
  127.5 13.2 %collective-permute-start.17 = (bf16[448,384]{1,0:T(8,128)(2,1)S(1)}, bf16[448,384]{1,0:T(8,128)(2,1)S(1)}, u32[]{:S(2)}, u32[]{:S(2)}) collective-permute-start(bf16[448,384]{1,0:T(8,128)(2,1)S(1)} %combine.1), channel_id=1, source_target_pairs={{0,2},{1,3},{2,0},{3,1},{4,6},{5,7},{6,4},{7,5},{8,10},{9,11},{10,... | collective-permute-start | bytes 1032200 | tf_op jit(solution)/shard_map/ppermute | solution.py:241
  128.4 13.3 %collective-permute-start.18 = (bf16[448,384]{1,0:T(8,128)(2,1)S(1)}, bf16[448,384]{1,0:T(8,128)(2,1)}, u32[]{:S(2)}, u32[]{:S(2)}) collective-permute-start(bf16[448,384]{1,0:T(8,128)(2,1)S(1)} %combine.1), channel_id=1, source_target_pairs={{0,3},{1,0},{2,1},{3,2},{4,7},{5,4},{6,5},{7,6},{8,11},{9,8},{10,9... | collective-permute-start | bytes 1032200 | tf_op jit(solution)/shard_map/ppermute | solution.py:241
  135.8 8.2 %copy-start.5 = (bf16[1536,1536]{1,0:T(8,128)(2,1)}, bf16[1536,1536]{1,0:T(8,128)(2,1)S(1)}, u32[]{:S(2)}) copy-start(bf16[1536,1536]{1,0:T(8,128)(2,1)S(1)} %pad_maximum_fusion) | copy-start | bytes 14155780
  144.0 28.8 %collective-permute-start.22 = (bf16[448,768]{1,0:T(8,128)(2,1)S(1)}, bf16[448,768]{1,0:T(8,128)(2,1)S(1)}, u32[]{:S(2)}, u32[]{:S(2)}) collective-permute-start(bf16[448,768]{1,0:T(8,128)(2,1)S(1)} %fusion.4), channel_id=1, source_target_pairs={{0,4},{4,0},{1,5},{5,1},{2,6},{6,2},{3,7},{7,3},{8,12},{12,8},{9,1... | collective-permute-start | bytes 2064392 | tf_op jit(solution)/shard_map/ppermute | solution.py:241
  157.7 3.4 %collective-permute-start.1 = (s32[1]{0:T(128)}, s32[1]{0:T(128)}, u32[]{:S(2)}, u32[]{:S(2)}) collective-permute-start(s32[1]{0:T(128)} %param.14), channel_id=1, source_target_pairs={{0,248},{8,0},{16,8},{24,16},{32,24},{40,32},{48,40},{56,48},{64,5... | collective-permute-start | bytes 20 | tf_op jit(solution)/shard_map/ppermute | solution.py:241
